TPU v7x, 32 devices: a whole 2x2x4 slice. The times are simulated.
32 devices in a mesh: dp: 16 (over z, x, core), tensor: 2 (over y).
Axes of the slice: x: 2, y: 2, z: 4, core: 2. Of those that a mesh axis runs over, the one named last changes fastest.
Arguments:
- tokens: bfloat16 [64, 502, 768], P('dp', 'tensor'), may hold values from -6 to 6
- slot_position: int32 [64], P('dp'), may hold values from -1 to 3, as said below
- cotangent: bfloat16 [64, 502, 768], P('dp', 'tensor'), may hold values from -6 to 6
- attention: float32 [4, 768, 768], P(None, 'dp', 'tensor'), may hold values from -4 to 4, as said below
- feedforward: float32 [2, 768, 3072], P(None, None, ('dp', 'tensor')), may hold values from -0.21875 to 0.21875
- vectors: float32 [16896], P(('dp', 'tensor')), may hold values from -6 to 6, as said below
- attn_momentum: float32 [4, 768, 768], P(None, 'dp', 'tensor'), may hold values from -2 to 2, as said below
- ffn_momentum: float32 [2, 768, 3072], P(None, None, ('dp', 'tensor')), may hold values from -3 to 3
- vec_momentum: float32 [16896], P(('dp', 'tensor')), may hold values from -3 to 3
- attn_average: float32 [4, 768, 768], P(None, 'dp', 'tensor'), may hold values from -4 to 4, as said below
- ffn_average: float32 [2, 768, 3072], P(None, None, ('dp', 'tensor')), may hold values from -0.21875 to 0.21875
- vec_average: float32 [16896], P(('dp', 'tensor')), may hold values from -6 to 6, as said below
Outputs:
- activations: bfloat16 [64, 502, 768], P('dp', 'tensor')
- token_grad: bfloat16 [64, 502, 768], P('dp', 'tensor')
- momentum_attn: float32 [4, 768, 768], P(None, 'dp', 'tensor')
- momentum_ffn: float32 [2, 768, 3072], P(None, None, ('dp', 'tensor'))
- momentum_vec: float32 [16896], P(('dp', 'tensor'))
- updated_attn: float32 [4, 768, 768], P(None, 'dp', 'tensor')
- updated_ffn: float32 [2, 768, 3072], P(None, None, ('dp', 'tensor'))
- updated_vec: float32 [16896], P(('dp', 'tensor'))
- averaged_attn: float32 [4, 768, 768], P(None, 'dp', 'tensor')
- averaged_ffn: float32 [2, 768, 3072], P(None, None, ('dp', 'tensor'))
- averaged_vec: float32 [16896], P(('dp', 'tensor'))
Inputs may be any that keep to these rules, and one draw needn't show every extreme that they name: `slot_position`: each bucket of 4 slots holds whole sequences one after another from its first slot: a slot holds its segment's place in its sequence, a sequence has 2 to 4 segments in consecutive slots starting at place 0, and the slots after a bucket's last sequence hold -1. Some bucket begins with a sequence of 4 segments. `attention`: entries of mean 0; the output projection's entries are larger than the others. `attn_momentum`: no entry is 0. `vectors`: gains near 1, biases of mean 0, initial memory of order one. `attn_average`: drawn by the same law as the attention weights. `vec_average`: drawn by the same law as vectors.
All inputs are finite; a program needn't handle non-finite values.
Results may differ from a plain program's by a relative error of at most 0.023.
Values may be sent and summed in bfloat16 or wider, within the bound.
A program may use at most 256 MiB of HBM per device.

v0:
```python
import math

import jax
import jax.numpy as jnp
from jax import lax
from jax.sharding import PartitionSpec as P

D = 768
HEADS = 12
DH = 64
FF = 3072
MEM = 10
SLOTS = 4
ROWS = 522
NVEC = 22


EPSILON = 1e-05
MOMENTUM = 0.9
AVERAGE_DECAY = 0.75
ATTENTION_RATE = 0.06
FEEDFORWARD_RATE = 0.02
VECTOR_RATE = 0.1
MASK_VALUE = -1e30


def passed_along(value, axis, steps):
    count = lax.axis_size(axis)
    leading, last = (max(0, -steps), min(count, count - steps))
    return lax.ppermute(value, axis, [(source, source + steps) for source in range(leading, last)])


def layer_norm(rows, norm_gain, norm_shift):
    center = rows - jnp.mean(rows, axis=-1, keepdims=True)
    spread = jnp.mean(center * center, axis=-1, keepdims=True)
    return center * lax.rsqrt(spread + EPSILON) * norm_gain + norm_shift


def exact_gelu(inputs):
    return jax.nn.gelu(inputs, approximate=False)


def fetch_forward(attention, feedforward, vectors):
    attn_full = lax.all_gather(attention.astype(jnp.bfloat16), "dp", axis=1, tiled=True)
    ffn_full, table_full = (
        lax.all_gather(feedforward.astype(jnp.bfloat16), ("dp", "tensor"), axis=2, tiled=True),
        lax.all_gather(
            vectors.astype(jnp.bfloat16).reshape(1, 1, -1), ("dp", "tensor"), axis=2, tiled=True
        ),
    )
    return (attn_full, ffn_full, table_full.reshape(-1))


def unpack(fetched, tensor_side, columns):
    attn_full, ffn_full, table_full = fetched
    table_rows = table_full.reshape(NVEC, D)
    table = table_rows.astype(jnp.float32)
    query_bias = lax.dynamic_slice_in_dim(table[0], tensor_side * columns, columns)
    value_bias = lax.dynamic_slice_in_dim(table[1], tensor_side * columns, columns)
    input_bias = jnp.stack([query_bias, jnp.zeros_like(query_bias), value_bias])
    up_bias = table[8 : 8 + FF // D].reshape(FF)
    memory_init = table_rows[8 + FF // D :]
    return (
        attn_full[:3],
        attn_full[3],
        ffn_full[0],
        ffn_full[1],
        table,
        input_bias,
        up_bias,
        memory_init,
    )


def update(gradient, momentum, weight, average, rate, grad_scale):
    scaled = gradient * grad_scale
    moment = MOMENTUM * momentum + scaled
    weight_new = weight - rate * (scaled + MOMENTUM * moment)
    return (moment, weight_new, AVERAGE_DECAY * average + (1.0 - AVERAGE_DECAY) * weight_new)


def on_device(
    tokens,
    slot_position,
    cotangent,
    attention,
    feedforward,
    vectors,
    attn_momentum,
    ffn_momentum,
    vec_momentum,
    attn_average,
    ffn_average,
    vec_average,
):
    tensor_side = lax.axis_index("tensor")
    head_count = HEADS // lax.axis_size("tensor")
    columns = head_count * DH
    half_rows = tokens.shape[1]
    local_count = half_rows + MEM
    score_scale = 1.0 / math.sqrt(DH)
    row_ids = lax.broadcasted_iota(jnp.int32, (ROWS, ROWS), 0)
    col_ids = lax.broadcasted_iota(jnp.int32, (ROWS, ROWS), 1)
    causal = (row_ids >= col_ids)[None]
    unpacked = unpack(fetch_forward(attention, feedforward, vectors), tensor_side, columns)
    (
        input_weights,
        output_weight,
        up_weight,
        down_weight,
        table,
        input_bias,
        up_bias,
        memory_init,
    ) = unpacked

    def forward_slot(memory, inputs):
        segment_tokens, segment_place = inputs
        memory_in = jnp.where(segment_place == 0, memory_init, memory)
        local_rows = jnp.where(
            tensor_side == 0,
            jnp.concatenate([memory_in, segment_tokens], axis=0),
            jnp.concatenate([segment_tokens, memory_in], axis=0),
        )
        all_rows = lax.all_gather(local_rows, "tensor", axis=0, tiled=True)
        projected = (
            jnp.einsum("rd,kdc->rkc", all_rows, input_weights, preferred_element_type=jnp.float32)
            + input_bias
        ).astype(jnp.bfloat16)
        split_heads = projected.reshape(ROWS, 3, head_count, DH)
        raw_scores = jnp.einsum(
            "qhd,khd->hqk", split_heads[:, 0], split_heads[:, 1], preferred_element_type=jnp.float32
        )
        scores = jnp.where(causal, raw_scores * score_scale, MASK_VALUE)
        row_max = jnp.max(scores, axis=-1, keepdims=True)
        exponent = jnp.exp(scores - row_max)
        row_total = jnp.sum(exponent, axis=-1, keepdims=True)
        attend = (exponent / row_total).astype(jnp.bfloat16)
        log_total = row_max + jnp.log(row_total)
        context = (
            jnp.einsum(
                "hqk,khd->qhd", attend, split_heads[:, 2], preferred_element_type=jnp.float32
            )
            .astype(jnp.bfloat16)
            .reshape(ROWS, columns)
        )
        branch = (
            lax.psum_scatter(
                jnp.einsum(
                    "rc,oc->ro", context, output_weight, preferred_element_type=jnp.float32
                ).astype(jnp.bfloat16),
                "tensor",
                scatter_dimension=0,
                tiled=True,
            ).astype(jnp.float32)
            + table[2]
        )
        pre_norm = local_rows.astype(jnp.float32) + branch
        hidden = layer_norm(pre_norm, table[3], table[4]).astype(jnp.bfloat16)
        upward = jnp.dot(hidden, up_weight, preferred_element_type=jnp.float32) + up_bias
        active = exact_gelu(upward).astype(jnp.bfloat16)
        downward = (
            jnp.einsum("rf,df->rd", active, down_weight, preferred_element_type=jnp.float32)
            + table[5]
        )
        second = hidden.astype(jnp.float32) + downward
        output = layer_norm(second, table[6], table[7]).astype(jnp.bfloat16)
        own_memory = output[local_count - MEM :]
        other_memory = passed_along(own_memory, "tensor", -1)
        next_memory = jnp.where(tensor_side == 0, other_memory, own_memory)
        token_rows = jnp.where(tensor_side == 0, output[MEM:], output[:half_rows])
        token_rows = jnp.where(segment_place >= 0, token_rows, jnp.zeros_like(token_rows))
        stored = (all_rows, projected, log_total, context, pre_norm, hidden, upward, active, second)
        return (next_memory, (token_rows, stored))

    memory_start = jnp.zeros((MEM, D), jnp.bfloat16)
    _, (activations, stored_all) = lax.scan(forward_slot, memory_start, (tokens, slot_position))

    def backward_slot(carry, inputs):
        memory_grad, sums = carry
        stored, segment_place, segment_cot = inputs
        all_rows, projected, log_total, kept_context, pre_norm, hidden, upward, active, second = (
            stored
        )
        slot_live = segment_place >= 0
        token_cot = jnp.where(slot_live, segment_cot.astype(jnp.float32), 0.0)
        zero_rows = jnp.zeros((MEM, D), jnp.float32)
        out_grad = jnp.where(
            tensor_side == 0,
            jnp.concatenate([zero_rows, token_cot], axis=0),
            jnp.concatenate([token_cot, memory_grad], axis=0),
        )
        second_pull = jax.vjp(layer_norm, second, table[6], table[7])[1]
        second_grad, gain_late, shift_late = second_pull(out_grad)
        down_grad = second_grad.astype(jnp.bfloat16)
        down_weight_grad = jnp.einsum(
            "rd,rf->df", down_grad, active, preferred_element_type=jnp.float32
        )
        active_grad = jnp.dot(down_grad, down_weight, preferred_element_type=jnp.float32)
        gelu_pull = jax.vjp(exact_gelu, upward)[1]
        upward_grad = gelu_pull(active_grad)[0].astype(jnp.bfloat16)
        up_weight_grad = jnp.einsum(
            "rd,rf->df", hidden, upward_grad, preferred_element_type=jnp.float32
        )
        hidden_grad = second_grad + jnp.einsum(
            "rf,df->rd", upward_grad, up_weight, preferred_element_type=jnp.float32
        )
        first_pull = jax.vjp(layer_norm, pre_norm, table[3], table[4])[1]
        pre_grad, gain_early, shift_early = first_pull(hidden_grad)
        branch_grad = pre_grad.astype(jnp.bfloat16)
        all_branch = lax.all_gather(branch_grad, "tensor", axis=0, tiled=True)
        output_weight_grad = jnp.einsum(
            "ro,rc->oc", all_branch, kept_context, preferred_element_type=jnp.float32
        )
        context_grad = (
            jnp.dot(all_branch, output_weight, preferred_element_type=jnp.float32)
            .astype(jnp.bfloat16)
            .reshape(ROWS, head_count, DH)
        )
        split_heads = projected.reshape(ROWS, 3, head_count, DH)
        raw_scores = jnp.einsum(
            "qhd,khd->hqk", split_heads[:, 0], split_heads[:, 1], preferred_element_type=jnp.float32
        )
        scores = jnp.where(causal, raw_scores * score_scale, MASK_VALUE)
        attend = jnp.exp(scores - log_total)
        attend_grad = jnp.einsum(
            "qhd,khd->hqk", context_grad, split_heads[:, 2], preferred_element_type=jnp.float32
        )
        value_grad = jnp.einsum(
            "hqk,qhd->khd",
            attend.astype(jnp.bfloat16),
            context_grad,
            preferred_element_type=jnp.float32,
        ).astype(jnp.bfloat16)
        row_inner = jnp.sum(attend_grad * attend, axis=-1, keepdims=True)
        raw_grad = (attend * (attend_grad - row_inner) * score_scale).astype(jnp.bfloat16)
        query_grad = jnp.einsum(
            "hqk,khd->qhd", raw_grad, split_heads[:, 1], preferred_element_type=jnp.float32
        ).astype(jnp.bfloat16)
        key_grad = jnp.einsum(
            "hqk,qhd->khd", raw_grad, split_heads[:, 0], preferred_element_type=jnp.float32
        ).astype(jnp.bfloat16)
        input_grad = jnp.stack([query_grad, key_grad, value_grad], axis=1).reshape(ROWS, 3, columns)
        input_weight_grad = jnp.einsum(
            "rd,rkc->kdc", all_rows, input_grad, preferred_element_type=jnp.float32
        )
        bias_sums = jnp.sum(input_grad, axis=0, dtype=jnp.float32)
        rows_grad = pre_grad + lax.psum_scatter(
            jnp.einsum(
                "rkc,kdc->rd", input_grad, input_weights, preferred_element_type=jnp.float32
            ).astype(jnp.bfloat16),
            "tensor",
            scatter_dimension=0,
            tiled=True,
        ).astype(jnp.float32)
        own_grad = jnp.where(tensor_side == 0, rows_grad[:MEM], rows_grad[local_count - MEM :])
        other_grad = passed_along(own_grad, "tensor", 1)
        carry_grad = jnp.where(segment_place > 0, own_grad + other_grad, 0.0)
        init_grad = jnp.where(segment_place == 0, own_grad, 0.0)
        token_grad = jnp.where(tensor_side == 0, rows_grad[MEM:], rows_grad[:half_rows])
        token_grad = jnp.where(slot_live, token_grad, 0.0).astype(jnp.bfloat16)
        empty_row = jnp.zeros((D,), jnp.float32)
        query_part = lax.dynamic_update_slice_in_dim(
            empty_row, bias_sums[0], tensor_side * columns, 0
        )
        value_part = lax.dynamic_update_slice_in_dim(
            empty_row, bias_sums[2], tensor_side * columns, 0
        )
        leading = jnp.stack(
            [
                query_part,
                value_part,
                jnp.sum(branch_grad, axis=0, dtype=jnp.float32),
                gain_early,
                shift_early,
                jnp.sum(down_grad, axis=0, dtype=jnp.float32),
                gain_late,
                shift_late,
            ]
        )
        small_grad = jnp.concatenate(
            [
                leading,
                jnp.sum(upward_grad, axis=0, dtype=jnp.float32).reshape(FF // D, D),
                init_grad,
            ],
            axis=0,
        )
        terms = (
            input_weight_grad,
            output_weight_grad,
            up_weight_grad,
            down_weight_grad,
            small_grad,
        )
        sums = jax.tree.map(jnp.add, sums, terms)
        return ((carry_grad, sums), token_grad)

    zero_sums = (
        jnp.zeros((3, D, columns), jnp.float32),
        jnp.zeros((D, output_weight.shape[1]), jnp.float32),
        jnp.zeros((D, FF), jnp.float32),
        jnp.zeros((D, FF), jnp.float32),
        jnp.zeros((NVEC, D), jnp.float32),
    )
    start_carry = (jnp.zeros((MEM, D), jnp.float32), zero_sums)
    (_, sums), token_grads = lax.scan(
        backward_slot, start_carry, (stored_all, slot_position, cotangent), reverse=True
    )
    output_terms = sums[1]
    attn_terms = jnp.concatenate([sums[0], output_terms[None]], axis=0)
    attn_grad = lax.psum_scatter(attn_terms, "dp", scatter_dimension=1, tiled=True)
    ffn_terms = jnp.stack([sums[2], sums[3]])
    ffn_grad, table_grad = (
        lax.psum_scatter(ffn_terms, ("dp", "tensor"), scatter_dimension=2, tiled=True),
        lax.psum_scatter(
            sums[4].reshape(1, 1, NVEC * D), ("dp", "tensor"), scatter_dimension=2, tiled=True
        ),
    )
    grad_scale = 1.0 / math.sqrt(lax.axis_size("dp") * SLOTS * ROWS)
    attn_new = update(attn_grad, attn_momentum, attention, attn_average, ATTENTION_RATE, grad_scale)
    ffn_new = update(ffn_grad, ffn_momentum, feedforward, ffn_average, FEEDFORWARD_RATE, grad_scale)
    vec_new = update(
        table_grad.reshape(-1), vec_momentum, vectors, vec_average, VECTOR_RATE, grad_scale
    )
    return (
        activations,
        token_grads,
        attn_new[0],
        ffn_new[0],
        vec_new[0],
        attn_new[1],
        ffn_new[1],
        vec_new[1],
        attn_new[2],
        ffn_new[2],
        vec_new[2],
    )


def solution(mesh):
    placed = (
        P("dp", "tensor", None),
        P("dp"),
        P("dp", "tensor", None),
        P(None, "dp", "tensor"),
        P(None, None, ("dp", "tensor")),
        P(("dp", "tensor")),
        P(None, "dp", "tensor"),
        P(None, None, ("dp", "tensor")),
        P(("dp", "tensor")),
        P(None, "dp", "tensor"),
        P(None, None, ("dp", "tensor")),
        P(("dp", "tensor")),
    )
    return jax.shard_map(
        on_device,
        mesh=mesh,
        in_specs=placed,
        out_specs=(
            P("dp", "tensor", None),
            P("dp", "tensor", None),
            P(None, "dp", "tensor"),
            P(None, None, ("dp", "tensor")),
            P(("dp", "tensor")),
            P(None, "dp", "tensor"),
            P(None, None, ("dp", "tensor")),
            P(("dp", "tensor")),
            P(None, "dp", "tensor"),
            P(None, None, ("dp", "tensor")),
            P(("dp", "tensor")),
        ),
        check_vma=False,
    )
```

profile of v0, /device:TPU:1, one launch (start us, length us, event | category | flops | bytes accessed | tf_op | source)
XLA Modules:
  0.0 1480.2 jit_solution(15273789305288793623)
XLA Ops:
  12.4 41.9 %all-reduce.1 = bf16[16896]{0:T(1024)(128)(2,1)S(1)} all-reduce(bf16[16896]{0:T(1024)(128)(2,1)S(1)} %dynamic-update-slice), channel_id=2, replica_groups=mesh['dp'=16,'tensor'=2] {'dp','tensor'}, use_global_device_ids=true, to_apply=%add.1 | all-reduce | flops 16896 | bytes 67584
  65.8 74.4 %all-gather.15.cloned.1.call-done = bf16[2,768,3072]{1,0,2:T(2,128)(2,1)} async-done(((bf16[2,768,96]{1,0,2:T(2,128)(2,1)}), bf16[2,768,3072]{1,0,2:T(2,128)(2,1)}) %all-gather.15.cloned.1.call-update) | async-done | bytes 9437200 | tf_op jit(solution)/shard_map/all_gather | solution.py:46
  140.3 19.1 %fusion.134 = (bf16[1,768,3072]{1,0,2:T(2,128)(2,1)}, bf16[1,768,3072]{1,0,2:T(2,128)(2,1)}) fusion(bf16[2,768,3072]{1,0,2:T(2,128)(2,1)} %all-gather.15.cloned.1.call-done), kind=kLoop, calls=%fused_computation.235 | loop fusion | bytes 18874368 | tf_op jit(solution)/shard_map/slice | solution.py:67
  159.4 19.8 %copy.117 = bf16[1,768,3072]{2,1,0:T(8,128)(2,1)} copy(bf16[1,768,3072]{1,0,2:T(2,128)(2,1)} %get-tuple-element.1374) | data formatting | bytes 9437184
  179.2 19.7 %copy.118 = bf16[1,768,3072]{2,1,0:T(8,128)(2,1)} copy(bf16[1,768,3072]{1,0,2:T(2,128)(2,1)} %get-tuple-element.1373) | data formatting | bytes 9437184
  200.2 271.3 %while.62 = (s32[]{:T(128)}, bf16[10,768]{1,0:T(8,128)(2,1)S(1)}, bf16[4,251,768]{2,1,0:T(8,128)(2,1)}, bf16[4,522,768]{2,1,0:T(8,128)(2,1)}, bf16[4,522,3,384]{...) while((s32[]{:T(128)}, bf16[10,768]{1,0:T(8,128)(2,1)S(1)}, ...), condition=%wide.wide.region_8.9_spmd.clone, body=%wide.wide.region_0.8_spmd.clone.sunk | while | flops 4212270848 | bytes 97532952 | solution.py:177
  228.6 12.5 fusion.263
  251.2 11.8 bitcast_dynamic-update-slice_fusion.20
  318.9 11.8 bitcast_dynamic-update-slice_fusion.20
  450.4 11.8 bitcast_dynamic-update-slice_fusion.20
  472.8 532.5 %while.61 = (s32[]{:T(128)}, f32[10,768]{1,0:T(8,128)}, f32[3,768,384]{1,2,0:T(8,128)}, f32[768,384]{1,0:T(8,128)}, f32[768,3072]{1,0:T(8,128)}, /*index=5*/f32[...) while((s32[]{:T(128)}, f32[10,768]{1,0:T(8,128)}, ...), condition=%wide.region_28.29_spmd.clone, body=%wide.region_9.28_spmd.clone.sunk | while | flops 8568051712 | bytes 325018720 | solution.py:307
  535.1 16.5 %fusion.247 = bf16[6,64,522]{2,1,0:T(8,128)(2,1)} fusion(f32[6,522,522]{1,2,0:T(8,128)} %fusion.246, f32[6,522,522]{1,2,0:T(8,128)} %copy-done, f32[6,522]{1,0:T(8,128)S(1)} %dynamic-slice_bitcast_fusion.7, pred[522,522]{0,1:T(8,128)(4,1)S(1)} %copy-done.16, bf16[522,3,6,64]{0,3,2,1:T(8,128)(2,1)S(1)} %bitcast.404), kind=kOutput, calls=%fused_computation.137.clone.1 | convolution fusion | flops 227455760 | bytes 34049536 | tf_op jit(solution)/shard_map/while/body/eval_jaxpr/hqk,qhd->khd/dot_general | solution.py:240
  551.6 16.5 %fusion.248 = bf16[6,64,522]{2,1,0:T(8,128)(2,1)} fusion(f32[6,522,522]{1,2,0:T(8,128)} %fusion.246, f32[6,522,522]{1,2,0:T(8,128)} %copy-done, f32[6,522]{1,0:T(8,128)S(1)} %dynamic-slice_bitcast_fusion.7, pred[522,522]{0,1:T(8,128)(4,1)S(1)} %copy-done.16, bf16[522,3,6,64]{0,3,2,1:T(8,128)(2,1)S(1)} %bitcast.405), kind=kOutput, calls=%fused_computation.136.clone.1 | convolution fusion | flops 227455760 | bytes 34049536 | tf_op jit(solution)/shard_map/while/body/eval_jaxpr/hqk,khd->qhd/dot_general | solution.py:237
  661.1 16.5 %fusion.247 = bf16[6,64,522]{2,1,0:T(8,128)(2,1)} fusion(f32[6,522,522]{1,2,0:T(8,128)} %fusion.246, f32[6,522,522]{1,2,0:T(8,128)} %copy-done, f32[6,522]{1,0:T(8,128)S(1)} %dynamic-slice_bitcast_fusion.7, pred[522,522]{0,1:T(8,128)(4,1)S(1)} %copy-done.16, bf16[522,3,6,64]{0,3,2,1:T(8,128)(2,1)S(1)} %bitcast.404), kind=kOutput, calls=%fused_computation.137.clone.1 | convolution fusion | flops 227455760 | bytes 34049536 | tf_op jit(solution)/shard_map/while/body/eval_jaxpr/hqk,qhd->khd/dot_general | solution.py:240
  677.6 16.5 %fusion.248 = bf16[6,64,522]{2,1,0:T(8,128)(2,1)} fusion(f32[6,522,522]{1,2,0:T(8,128)} %fusion.246, f32[6,522,522]{1,2,0:T(8,128)} %copy-done, f32[6,522]{1,0:T(8,128)S(1)} %dynamic-slice_bitcast_fusion.7, pred[522,522]{0,1:T(8,128)(4,1)S(1)} %copy-done.16, bf16[522,3,6,64]{0,3,2,1:T(8,128)(2,1)S(1)} %bitcast.405), kind=kOutput, calls=%fused_computation.136.clone.1 | convolution fusion | flops 227455760 | bytes 34049536 | tf_op jit(solution)/shard_map/while/body/eval_jaxpr/hqk,khd->qhd/dot_general | solution.py:237
  791.0 16.5 %fusion.247 = bf16[6,64,522]{2,1,0:T(8,128)(2,1)} fusion(f32[6,522,522]{1,2,0:T(8,128)} %fusion.246, f32[6,522,522]{1,2,0:T(8,128)} %copy-done, f32[6,522]{1,0:T(8,128)S(1)} %dynamic-slice_bitcast_fusion.7, pred[522,522]{0,1:T(8,128)(4,1)S(1)} %copy-done.16, bf16[522,3,6,64]{0,3,2,1:T(8,128)(2,1)S(1)} %bitcast.404), kind=kOutput, calls=%fused_computation.137.clone.1 | convolution fusion | flops 227455760 | bytes 34049536 | tf_op jit(solution)/shard_map/while/body/eval_jaxpr/hqk,qhd->khd/dot_general | solution.py:240
  807.5 16.5 %fusion.248 = bf16[6,64,522]{2,1,0:T(8,128)(2,1)} fusion(f32[6,522,522]{1,2,0:T(8,128)} %fusion.246, f32[6,522,522]{1,2,0:T(8,128)} %copy-done, f32[6,522]{1,0:T(8,128)S(1)} %dynamic-slice_bitcast_fusion.7, pred[522,522]{0,1:T(8,128)(4,1)S(1)} %copy-done.16, bf16[522,3,6,64]{0,3,2,1:T(8,128)(2,1)S(1)} %bitcast.405), kind=kOutput, calls=%fused_computation.136.clone.1 | convolution fusion | flops 227455760 | bytes 34049536 | tf_op jit(solution)/shard_map/while/body/eval_jaxpr/hqk,khd->qhd/dot_general | solution.py:237
  921.0 16.5 %fusion.247 = bf16[6,64,522]{2,1,0:T(8,128)(2,1)} fusion(f32[6,522,522]{1,2,0:T(8,128)} %fusion.246, f32[6,522,522]{1,2,0:T(8,128)} %copy-done, f32[6,522]{1,0:T(8,128)S(1)} %dynamic-slice_bitcast_fusion.7, pred[522,522]{0,1:T(8,128)(4,1)S(1)} %copy-done.16, bf16[522,3,6,64]{0,3,2,1:T(8,128)(2,1)S(1)} %bitcast.404), kind=kOutput, calls=%fused_computation.137.clone.1 | convolution fusion | flops 227455760 | bytes 34049536 | tf_op jit(solution)/shard_map/while/body/eval_jaxpr/hqk,qhd->khd/dot_general | solution.py:240
  937.5 16.5 %fusion.248 = bf16[6,64,522]{2,1,0:T(8,128)(2,1)} fusion(f32[6,522,522]{1,2,0:T(8,128)} %fusion.246, f32[6,522,522]{1,2,0:T(8,128)} %copy-done, f32[6,522]{1,0:T(8,128)S(1)} %dynamic-slice_bitcast_fusion.7, pred[522,522]{0,1:T(8,128)(4,1)S(1)} %copy-done.16, bf16[522,3,6,64]{0,3,2,1:T(8,128)(2,1)S(1)} %bitcast.405), kind=kOutput, calls=%fused_computation.136.clone.1 | convolution fusion | flops 227455760 | bytes 34049536 | tf_op jit(solution)/shard_map/while/body/eval_jaxpr/hqk,khd->qhd/dot_general | solution.py:237
  1010.4 15.6 %reshape.303 = f32[1,1,16896]{1,0,2:T(1,128)} reshape(f32[22,768]{1,0:T(8,128)S(1)} %copy-done.22) | data formatting | bytes 135168 | tf_op jit(solution)/shard_map/reshape | solution.py:317
  1051.2 14.9 %pad_maximum_fusion.3 = f32[2,768,3072]{1,2,0:T(8,128)} fusion(f32[1,768,3072]{1,2,0:T(8,128)} %bitcast.413, f32[1,768,3072]{1,2,0:T(8,128)} %bitcast.414), kind=kLoop, calls=%fused_computation.211 | loop fusion | flops 4718592 | bytes 37748736 | tf_op jit(solution)/shard_map/stack | solution.py:313
  1072.3 108.1 %reduce-scatter.14.cloned.1.call-done = f32[528,1]{1,0:T(8,128)} async-done(((f32[16896,1]{1,0:T(8,128)}), f32[528,1]{1,0:T(8,128)}) %reduce-scatter.14.cloned.1.call-update) | async-done | bytes 2128
  1182.2 77.6 %reduce-scatter.10.cloned.1.call-done = f32[4,48,384]{2,1,0:T(8,128)} async-done(((f32[4,768,384]{2,1,0:T(8,128)}), f32[4,48,384]{2,1,0:T(8,128)}) %reduce-scatter.10.cloned.1.call-update) | async-done | bytes 294928 | tf_op jit(solution)/shard_map/reduce_scatter | solution.py:312
  1261.7 209.3 %reduce-scatter.12.cloned.1.call-done = f32[2,768,96]{1,2,0:T(8,128)} async-done(((f32[2,768,3072]{1,2,0:T(8,128)}), f32[2,768,96]{1,2,0:T(8,128)}) %reduce-scatter.12.cloned.1.call-update) | async-done | bytes 589840 | tf_op jit(solution)/shard_map/reduce_scatter | solution.py:315
  (776 shorter events, 646.9 us)
Async XLA Ops:
  7.2 53.8 %all-gather.13.cloned.1.call-start = ((), (), s32[]{:S(2)}) async-start(), calls=%async_computation.3 | async-start | bytes 2506752 | tf_op jit(solution)/shard_map/all_gather | solution.py:44
  9.0 131.2 %all-gather.15.cloned.1.call-start = ((), (), s32[]{:S(2)}) async-start(), calls=%async_computation.4 | async-start | bytes 9732096 | tf_op jit(solution)/shard_map/all_gather | solution.py:46
  11.3 1169.1 %reduce-scatter.14.cloned.1.call-start = ((), (), s32[]{:S(2)}) async-start(), calls=%async_computation.7 | async-start | bytes 8921088
  241.1 8.0 collective-permute-start.2
  265.5 6.9 collective-permute-start.3
  308.4 8.4 collective-permute-start.2
  333.1 7.0 collective-permute-start.3
  374.8 7.8 collective-permute-start.2
  398.9 6.8 collective-permute-start.3
  440.5 7.8 collective-permute-start.2
  464.6 6.8 collective-permute-start.3
  585.4 25.1 %collective-permute-start = (bf16[3,768]{1,0:T(4,128)(2,1)S(1)}, bf16[3,768]{1,0:T(4,128)(2,1)S(1)}, u32[]{:S(2)}, u32[]{:S(2)}) collective-permute-start(bf16[3,768]{1,0:T(4,128)(2,1)S(1)} %slice.352), channel_id=1, source_target_pairs={{0,1},{2,3},{4,5},{6,7},{8,9},{10,11},{12,13},{14,15},{16,17},{18,... | collective-permute-start | bytes 13832 | tf_op jit(solution)/shard_map/while
  611.9 2.5 collective-permute-start.1
  711.4 29.0 %collective-permute-start = (bf16[3,768]{1,0:T(4,128)(2,1)S(1)}, bf16[3,768]{1,0:T(4,128)(2,1)S(1)}, u32[]{:S(2)}, u32[]{:S(2)}) collective-permute-start(bf16[3,768]{1,0:T(4,128)(2,1)S(1)} %slice.352), channel_id=1, source_target_pairs={{0,1},{2,3},{4,5},{6,7},{8,9},{10,11},{12,13},{14,15},{16,17},{18,... | collective-permute-start | bytes 13832 | tf_op jit(solution)/shard_map/while
  741.8 2.5 collective-permute-start.1
  841.3 29.0 %collective-permute-start = (bf16[3,768]{1,0:T(4,128)(2,1)S(1)}, bf16[3,768]{1,0:T(4,128)(2,1)S(1)}, u32[]{:S(2)}, u32[]{:S(2)}) collective-permute-start(bf16[3,768]{1,0:T(4,128)(2,1)S(1)} %slice.352), channel_id=1, source_target_pairs={{0,1},{2,3},{4,5},{6,7},{8,9},{10,11},{12,13},{14,15},{16,17},{18,... | collective-permute-start | bytes 13832 | tf_op jit(solution)/shard_map/while
  871.8 2.5 collective-permute-start.1
  971.3 29.0 %collective-permute-start = (bf16[3,768]{1,0:T(4,128)(2,1)S(1)}, bf16[3,768]{1,0:T(4,128)(2,1)S(1)}, u32[]{:S(2)}, u32[]{:S(2)}) collective-permute-start(bf16[3,768]{1,0:T(4,128)(2,1)S(1)} %slice.352), channel_id=1, source_target_pairs={{0,1},{2,3},{4,5},{6,7},{8,9},{10,11},{12,13},{14,15},{16,17},{18,... | collective-permute-start | bytes 13832 | tf_op jit(solution)/shard_map/while
  1001.7 2.5 collective-permute-start.1
  1026.1 233.7 %reduce-scatter.10.cloned.1.call-start = ((), (), s32[]{:S(2)}) async-start(), calls=%async_computation.5 | async-start | bytes 5013504 | tf_op jit(solution)/shard_map/reduce_scatter | solution.py:312
  1031.9 439.1 %reduce-scatter.12.cloned.1.call-start = ((), (), s32[]{:S(2)}) async-start(), calls=%async_computation.6 | async-start | bytes 19464192 | tf_op jit(solution)/shard_map/reduce_scatter | solution.py:315
  1070.0 401.0 %copy-start.23 = (f32[2,768,96]{1,2,0:T(8,128)S(1)}, f32[2,768,96]{1,2,0:T(8,128)}, u32[]{:S(2)}) copy-start(f32[2,768,96]{1,2,0:T(8,128)} %param.20) | copy-start | bytes 1769476
  1070.0 401.0 %copy-start.30 = (f32[2,768,96]{1,2,0:T(8,128)S(1)}, f32[2,768,96]{1,2,0:T(8,128)}, u32[]{:S(2)}) copy-start(f32[2,768,96]{1,2,0:T(8,128)} %param.26) | copy-start | bytes 1769476
  1070.0 401.0 %copy-start.31 = (f32[2,768,96]{1,2,0:T(8,128)S(1)}, f32[2,768,96]{1,2,0:T(8,128)}, u32[]{:S(2)}) copy-start(f32[2,768,96]{1,2,0:T(8,128)} %param.23) | copy-start | bytes 1769476
  (132 other events, 1899.8 us)
Sparse Core Ops, SparseCore 0:
  10.8 44.9 all-gather.12
  59.3 80.9 all-gather.14
  1026.2 154.1 reduce-scatter.13
  1184.1 75.5 reduce-scatter.9
  1267.2 203.8 reduce-scatter.11
where the time goes:
time: 1490 us; the launch traced here: 1480 us
  waiting for transfers between devices  470 us (32%)
  matrix products  414 us (28%)
  local copies, waits for them, and re-layouts  217 us (15%)
  blocking collectives  195 us (13%)
  other arithmetic  104 us (7%)
  loops' own time  38.6 us (3%)
  starting transfers between devices  26.7 us (2%)
    reduce_scatter x1, waiting for transfers between devices, on_device(): lax.psum_scatter(ffn_terms, ('dp', 'tensor'), scatter_dimension=2, tiled=...  209 us
    unnamed x6, waiting for transfers between devices  108 us
    while x8, blocking collectives  85.1 us
    reduce_scatter x1, waiting for transfers between devices, on_device(): lax.psum_scatter(attn_terms, 'dp', scatter_dimension=1, tiled=True)  77.6 us
    all_gather x1, waiting for transfers between devices, fetch_forward(): lax.all_gather(feedforward.astype(jnp.bfloat16), ('dp', 'tensor'), axis=2...  74.4 us
    dot_general x4, matrix products, backward_slot(): jnp.einsum('hqk,khd->qhd', raw_grad, split_heads[:, 1], preferred_element...  66 us
    dot_general x4, matrix products, backward_slot(): jnp.einsum('hqk,qhd->khd', raw_grad, split_heads[:, 0], preferred_element...  66 us
    unnamed x40, local copies, waits for them, and re-layouts  54.5 us
  transfers between devices with their start and end apart: 21, of which 4 were waited for; matrix products, arithmetic and copies ran while one was open for 14% of the time, Pallas kernels for 0%

commit v1 on v0

v1 whole, which is shorter than its diff:
```python
import functools
import math

import jax
import jax.numpy as jnp
from jax import lax
from jax.experimental import pallas as pl
from jax.experimental.pallas import tpu as pltpu
from jax.sharding import PartitionSpec as P

D = 768
HEADS = 12
DH = 64
FF = 3072
MEM = 10
SLOTS = 4
ROWS = 522
NVEC = 22

HALF = D // 2
SEG = ROWS - MEM
THIN = 16
LOCAL = 2
TILE = 256

EPSILON = 1e-05
MOMENTUM = 0.9
AVERAGE_DECAY = 0.75
ATTENTION_RATE = 0.06
FEEDFORWARD_RATE = 0.02
VECTOR_RATE = 0.1
MASK_VALUE = -1e30
SCALE = 1.0 / math.sqrt(DH)

F32 = jnp.float32
BF16 = jnp.bfloat16
MIB = 1 << 20

QUERY_BIAS, VALUE_BIAS, OUT_BIAS, GAIN1, SHIFT1, DOWN_BIAS, GAIN2, SHIFT2, UP_BIAS = range(9)
FIRST_MEMORY = UP_BIAS + FF // D


def nn(a, b):
    return lax.dot_general(a, b, (((1,), (0,)), ((), ())), preferred_element_type=F32)


def nt(a, b):
    return lax.dot_general(a, b, (((1,), (1,)), ((), ())), preferred_element_type=F32)


def tn(a, b):
    return lax.dot_general(a, b, (((0,), (0,)), ((), ())), preferred_element_type=F32)


def normalized(rows):
    center = rows - jnp.mean(rows, axis=-1, keepdims=True)
    spread = jnp.mean(center * center, axis=-1, keepdims=True)
    inverse = lax.rsqrt(spread + EPSILON)
    return center * inverse, inverse


def normalized_back(grad, unit, inverse):
    mean_grad = jnp.mean(grad, axis=-1, keepdims=True)
    mean_along = jnp.mean(grad * unit, axis=-1, keepdims=True)
    return inverse * (grad - mean_grad - unit * mean_along)


def gelu_parts(u):
    size = jnp.abs(u)
    t = 1.0 / (1.0 + (0.3275911 / math.sqrt(2.0)) * size)
    bell = jnp.exp(-0.5 * u * u)
    poly = t * (
        0.5 * 0.254829592
        + t
        * (
            0.5 * -0.284496736
            + t * (0.5 * 1.421413741 + t * (0.5 * -1.453152027 + t * (0.5 * 1.061405429)))
        )
    )
    tail = poly * bell
    cdf = jnp.where(u < 0, tail, 1.0 - tail)
    return u * cdf, cdf + (u * (1.0 / math.sqrt(2.0 * math.pi))) * bell


def row_sum(block):
    return jnp.sum(block, axis=0, keepdims=True)


def params(limit=60, **more):
    return pltpu.CompilerParams(vmem_limit_bytes=limit * MIB, **more)


def once(shape, index):
    return pl.BlockSpec(shape, lambda *_: index, pipeline_mode=pl.Buffered(1))


ANY = pl.BlockSpec(memory_space=pl.ANY)
SMEM = pl.BlockSpec(memory_space=pltpu.SMEM)
VMEM = pl.BlockSpec(memory_space=pltpu.VMEM)


def sds(shape, dtype):
    return jax.ShapeDtypeStruct(shape, dtype)


def project_kernel(x_ref, w_ref, table_ref, q_ref, k_ref, v_ref):
    x = x_ref[0]
    for side in range(2):
        cols = slice(HALF * side, HALF * (side + 1))
        query = nn(x, w_ref[side, 0]) + table_ref[QUERY_BIAS : QUERY_BIAS + 1, cols]
        q_ref[0, :, cols] = (query * SCALE).astype(BF16)
        k_ref[0, :, cols] = nn(x, w_ref[side, 1]).astype(BF16)
        value = nn(x, w_ref[side, 2]) + table_ref[VALUE_BIAS : VALUE_BIAS + 1, cols]
        v_ref[0, :, cols] = value.astype(BF16)


def project(x, attn, table):
    rows = pl.BlockSpec((1, TILE, D), lambda s, i: (s, i, 0))
    return pl.pallas_call(
        project_kernel,
        grid=(LOCAL, SEG // TILE),
        in_specs=[rows, once((2, 3, D, HALF), (0, 0, 0, 0)), once((NVEC, D), (0, 0))],
        out_specs=[rows] * 3,
        out_shape=[sds((LOCAL, SEG, D), BF16)] * 3,
        compiler_params=params(),
    )(x, attn, table)


def head_masks():
    feature_head = lax.broadcasted_iota(jnp.int32, (1, D), 1) // DH
    return [feature_head == h for h in range(HEADS)]


def by_head(rows16, masks):
    zero = jnp.zeros_like(rows16)
    return jnp.concatenate([jnp.where(m, rows16, zero) for m in masks], axis=0)


def own_columns(blocks, masks):
    total = jnp.zeros((THIN, D), blocks.dtype)
    for h, m in enumerate(masks):
        total = jnp.where(m, blocks[THIN * h : THIN * (h + 1)], total)
    return total


def copies_of(key_mask_shape):
    row = lax.rem(lax.broadcasted_iota(jnp.int32, key_mask_shape, 0), THIN)
    key = lax.broadcasted_iota(jnp.int32, key_mask_shape, 1)
    return jnp.where((key < MEM) & (key <= row), 2.0, 1.0)


def chain_kernel(
    place_ref,
    flag_ref,
    start_ref,
    table_ref,
    attn_ref,
    ffn_ref,
    x_in,
    q_in,
    k_in,
    v_in,
    saved_d_in,
    saved_f_in,
    saved_s_in,
    x_ref,
    q_ref,
    k_ref,
    v_ref,
    saved_d_ref,
    saved_f_ref,
    saved_s_ref,
    memory_ref,
    wa,
    wf,
    xb,
    qb,
    kb,
    vb,
    save_d,
    save_f,
    save_s,
    sem_w,
    sem_x,
    sem_kv,
    sem_out,
):
    del x_in, q_in, k_in, v_in, saved_d_in, saved_f_in, saved_s_in
    active = flag_ref[0] > 0
    memory_ref[...] = start_ref[...]

    @pl.when(active)
    def _():
        loads = [
            pltpu.make_async_copy(attn_ref, wa, sem_w.at[0]),
            pltpu.make_async_copy(ffn_ref.at[0], wf.at[0], sem_w.at[1]),
            pltpu.make_async_copy(ffn_ref.at[1], wf.at[1], sem_w.at[2]),
        ]
        tiles = [
            pltpu.make_async_copy(x_ref.at[s, pl.ds(0, THIN)], xb.at[s], sem_x.at[s])
            for s in range(LOCAL)
        ]
        keys = [
            pltpu.make_async_copy(src.at[s], dst.at[s], sem_kv.at[2 * s + i])
            for s in range(LOCAL)
            for i, (src, dst) in enumerate(((k_ref, kb), (v_ref, vb)))
        ]
        for c in tiles + loads[:1] + keys + loads[1:]:
            c.start()
        masks = head_masks()
        memory_row = lax.broadcasted_iota(jnp.int32, (THIN, 1), 0) < MEM
        first = table_ref[FIRST_MEMORY:NVEC, :]
        first = jnp.concatenate([first, jnp.zeros((THIN - MEM, D), F32)], axis=0)
        row = lambda r: table_ref[r : r + 1, :]
        for s in range(LOCAL):
            tiles[s].wait()
            if s == 0:
                loads[0].wait()
            keys[2 * s].wait()
            keys[2 * s + 1].wait()
            memory = jnp.where(place_ref[s] == 0, first, memory_ref[...].astype(F32))
            x16 = jnp.where(memory_row, memory, xb[s].astype(F32)).astype(BF16)
            xb[s] = x16
            for side in range(2):
                cols = slice(HALF * side, HALF * (side + 1))
                query = nn(x16, wa[side, 0]) + table_ref[QUERY_BIAS : QUERY_BIAS + 1, cols]
                qb[s, :, cols] = (query * SCALE).astype(BF16)
                kb[s, 0:THIN, cols] = nn(x16, wa[side, 1]).astype(BF16)
                value = nn(x16, wa[side, 2]) + table_ref[VALUE_BIAS : VALUE_BIAS + 1, cols]
                vb[s, 0:THIN, cols] = value.astype(BF16)
            outs = [
                pltpu.make_async_copy(xb.at[s], x_ref.at[s, pl.ds(0, THIN)], sem_out.at[4 * s]),
                pltpu.make_async_copy(qb.at[s], q_ref.at[s, pl.ds(0, THIN)], sem_out.at[4 * s + 1]),
                pltpu.make_async_copy(
                    kb.at[s, pl.ds(0, THIN)], k_ref.at[s, pl.ds(0, THIN)], sem_out.at[4 * s + 2]
                ),
                pltpu.make_async_copy(
                    vb.at[s, pl.ds(0, THIN)], v_ref.at[s, pl.ds(0, THIN)], sem_out.at[4 * s + 3]
                ),
            ]
            for c in outs:
                c.start()

            def rest(s=s):
                q_heads = by_head(qb[s], masks)
                score = nt(q_heads, kb[s])
                top = jnp.max(score, axis=-1, keepdims=True)
                weight = jnp.exp(score - top) * copies_of(score.shape)
                total = jnp.sum(weight, axis=-1, keepdims=True)
                share = (weight / total).astype(BF16)
                log_total = top + jnp.log(total)
                context = own_columns(nn(share, vb[s]), masks).astype(BF16)
                branch = nt(context[:, :HALF], wa[0, 3]) + nt(context[:, HALF:], wa[1, 3])
                unit1, inverse1 = normalized(xb[s].astype(F32) + branch + row(OUT_BIAS))
                hidden = (unit1 * row(GAIN1) + row(SHIFT1)).astype(BF16)
                if s == 0:
                    loads[1].wait()
                up = nt(hidden, wf[0])
                up_bias = jnp.concatenate([row(UP_BIAS + i) for i in range(FF // D)], axis=1)
                active16, slope = gelu_parts(up + up_bias)
                active16 = active16.astype(BF16)
                if s == 0:
                    loads[2].wait()
                second = hidden.astype(F32) + nn(active16, wf[1]) + row(DOWN_BIAS)
                unit2, inverse2 = normalized(second)
                memory_ref[...] = (unit2 * row(GAIN2) + row(SHIFT2)).astype(BF16)
                save_d[s, 0] = hidden
                save_d[s, 1] = unit1.astype(BF16)
                save_d[s, 2] = unit2.astype(BF16)
                save_d[s, 3] = context
                save_f[s, 0] = active16
                save_f[s, 1] = slope.astype(BF16)
                wide = lambda v: jnp.broadcast_to(v, (v.shape[0], 128))
                save_s[s, 0 : HEADS * THIN] = wide(log_total)
                save_s[s, HEADS * THIN : HEADS * THIN + THIN] = wide(inverse1)
                save_s[s, HEADS * THIN + THIN :] = wide(inverse2)

            if s == LOCAL - 1:
                last_needed = flag_ref[1] > 0

                @pl.when(last_needed)
                def _():
                    rest()

                @pl.when(jnp.logical_not(last_needed))
                def _():
                    loads_done = (s != 0)
                    del loads_done
                    save_d[s] = jnp.zeros_like(save_d[s])
                    save_f[s] = jnp.zeros_like(save_f[s])
                    save_s[s] = jnp.zeros_like(save_s[s])
            else:
                rest()
            for c in outs:
                c.wait()
        saves = [
            pltpu.make_async_copy(save_d, saved_d_ref, sem_out.at[0]),
            pltpu.make_async_copy(save_f, saved_f_ref, sem_out.at[1]),
            pltpu.make_async_copy(save_s, saved_s_ref, sem_out.at[2]),
        ]
        for c in saves:
            c.start()
        for c in saves:
            c.wait()


SAVED = (
    sds((LOCAL, 4, THIN, D), BF16),
    sds((LOCAL, 2, THIN, FF), BF16),
    sds((LOCAL, HEADS * THIN + 2 * THIN, 128), F32),
)


def chain(place, flag, start, table, attn, ffn, x, q, k, v, saved):
    whole = sds((LOCAL, SEG, D), BF16)
    outs = pl.pallas_call(
        chain_kernel,
        in_specs=[SMEM, SMEM, VMEM, VMEM] + [ANY] * 9,
        out_specs=[ANY] * 7 + [VMEM],
        out_shape=[whole] * 4 + list(SAVED) + [sds((THIN, D), BF16)],
        input_output_aliases={6 + i: i for i in range(7)},
        scratch_shapes=[
            pltpu.VMEM((2, 4, D, HALF), BF16),
            pltpu.VMEM((2, FF, D), BF16),
            pltpu.VMEM((LOCAL, THIN, D), BF16),
            pltpu.VMEM((LOCAL, THIN, D), BF16),
            pltpu.VMEM((LOCAL, SEG, D), BF16),
            pltpu.VMEM((LOCAL, SEG, D), BF16),
            pltpu.VMEM((LOCAL, 4, THIN, D), BF16),
            pltpu.VMEM((LOCAL, 2, THIN, FF), BF16),
            pltpu.VMEM((LOCAL, HEADS * THIN + 2 * THIN, 128), F32),
            pltpu.SemaphoreType.DMA((3,)),
            pltpu.SemaphoreType.DMA((LOCAL,)),
            pltpu.SemaphoreType.DMA((2 * LOCAL,)),
            pltpu.SemaphoreType.DMA((4 * LOCAL,)),
        ],
        compiler_params=params(),
    )(place, flag, start, table, attn, ffn, x, q, k, v, *saved)
    return outs[:4], outs[4:7], outs[7]


def own_lanes(block, head):
    lane = lax.broadcasted_iota(jnp.int32, block.shape, 1)
    return jnp.where((lane < DH) == (head == 0), block, jnp.zeros_like(block))


def seen(score, first_query):
    key = lax.broadcasted_iota(jnp.int32, score.shape, 0)
    query = lax.broadcasted_iota(jnp.int32, score.shape, 1) + first_query
    return key <= query


def attend_kernel(q_ref, k_ref, v_ref, c_ref, log_ref):
    for part in range(SEG // TILE):
        rows = slice(TILE * part, TILE * (part + 1))
        keys = slice(0, TILE * (part + 1))
        contexts = []
        for head in range(2):
            score = nt(own_lanes(k_ref[0, keys], head), q_ref[0, rows])
            score = jnp.where(seen(score, TILE * part), score, MASK_VALUE)
            top = jnp.max(score, axis=0, keepdims=True)
            weight = jnp.exp(score - top)
            total = jnp.sum(weight, axis=0, keepdims=True)
            share = (weight * (1.0 / total)).astype(BF16)
            log_ref[0, 0, head : head + 1, rows] = top + jnp.log(total)
            contexts.append(tn(share, v_ref[0, keys]))
        lane = lax.broadcasted_iota(jnp.int32, contexts[0].shape, 1)
        c_ref[0, rows] = jnp.where(lane < DH, contexts[0], contexts[1]).astype(BF16)


PAIR = pl.BlockSpec((1, SEG, 2 * DH), lambda s, h: (s, 0, h))
PAIR_LOG = pl.BlockSpec((1, 1, 2, SEG), lambda s, h: (s, h, 0, 0))


def attend(q, k, v):
    return pl.pallas_call(
        attend_kernel,
        grid=(LOCAL, HEADS // 2),
        in_specs=[PAIR] * 3,
        out_specs=[PAIR, PAIR_LOG],
        out_shape=[sds((LOCAL, SEG, D), BF16), sds((LOCAL, HEADS // 2, 2, SEG), F32)],
        compiler_params=params(),
    )(q, k, v)


def attend_back_kernel(q_ref, k_ref, v_ref, dc_ref, log_ref, dq_ref, dk_ref, dv_ref):
    last = SEG // TILE
    key_terms, value_terms = [], []
    for head in range(2):
        key_sum, value_sum = [], []
        query_parts = []
        for part in range(last):
            rows = slice(TILE * part, TILE * (part + 1))
            keys = slice(0, TILE * (part + 1))
            q, dc = q_ref[0, rows], dc_ref[0, rows]
            k = k_ref[0, keys]
            score = nt(own_lanes(k, head), q)
            share = jnp.exp(score - log_ref[0, 0, head : head + 1, rows])
            share = jnp.where(seen(score, TILE * part), share, 0.0)
            share_grad = nt(own_lanes(v_ref[0, keys], head), dc)
            inner = jnp.sum(share_grad * share, axis=0, keepdims=True)
            score_grad = (share * (share_grad - inner)).astype(BF16)
            value_sum.append(nn(share.astype(BF16), dc))
            key_sum.append(nn(score_grad, q))
            query_parts.append(tn(score_grad, k))
        key_terms.append(key_sum)
        value_terms.append(value_sum)
        if head == 0:
            first_queries = query_parts
    for part in range(last):
        rows = slice(TILE * part, TILE * (part + 1))
        lane = lax.broadcasted_iota(jnp.int32, (TILE, 2 * DH), 1)
        pick = lambda a, b: jnp.where(lane < DH, a, b)
        dq_ref[0, rows] = (pick(first_queries[part], query_parts[part]) * SCALE).astype(BF16)
        for terms, out in ((key_terms, dk_ref), (value_terms, dv_ref)):
            total = None
            for later in range(part, last):
                term = pick(terms[0][later][rows], terms[1][later][rows])
                total = term if total is None else total + term
            out[0, rows] = total.astype(BF16)


def attend_back(q, k, v, dc, log_total):
    return pl.pallas_call(
        attend_back_kernel,
        grid=(LOCAL, HEADS // 2),
        in_specs=[PAIR] * 4 + [PAIR_LOG],
        out_specs=[PAIR] * 3,
        out_shape=[sds((LOCAL, SEG, D), BF16)] * 3,
        compiler_params=params(),
    )(q, k, v, dc, log_total)


def rows_kernel(
    x_ref,
    c_ref,
    cot_ref,
    wo_ref,
    wf_ref,
    table_ref,
    y_ref,
    h_ref,
    g_ref,
    du_ref,
    df_ref,
    da_ref,
    dc_ref,
    sums_ref,
    slope_ref,
):
    row = lambda r: table_ref[r : r + 1, :]

    @pl.when((pl.program_id(0) == 0) & (pl.program_id(1) == 0))
    def _():
        sums_ref[...] = jnp.zeros_like(sums_ref)

    def add(r, value):
        sums_ref[r : r + 1, :] += value

    c = c_ref[0]
    branch = nt(c[:, :HALF], wo_ref[0, 0]) + nt(c[:, HALF:], wo_ref[1, 0])
    unit1, inverse1 = normalized(x_ref[0].astype(F32) + branch + row(OUT_BIAS))
    hidden = (unit1 * row(GAIN1) + row(SHIFT1)).astype(BF16)
    h_ref[0] = hidden
    second = hidden.astype(F32) + row(DOWN_BIAS)
    for i in range(FF // D):
        cols = slice(D * i, D * (i + 1))
        up = nt(hidden, wf_ref[0, cols]) + row(UP_BIAS + i)
        active, slope = gelu_parts(up)
        active = active.astype(BF16)
        g_ref[0, :, cols] = active
        slope_ref[:, cols] = slope.astype(BF16)
        second = second + nn(active, wf_ref[1, cols])
    unit2, inverse2 = normalized(second)
    y_ref[0] = (unit2 * row(GAIN2) + row(SHIFT2)).astype(BF16)

    grad = cot_ref[0].astype(F32)
    add(GAIN2, row_sum(grad * unit2))
    add(SHIFT2, row_sum(grad))
    second_grad = normalized_back(grad * row(GAIN2), unit2, inverse2)
    down_grad = second_grad.astype(BF16)
    df_ref[0] = down_grad
    add(DOWN_BIAS, row_sum(down_grad.astype(F32)))
    hidden_grad = second_grad
    for i in range(FF // D):
        cols = slice(D * i, D * (i + 1))
        up_grad = (nt(down_grad, wf_ref[1, cols]) * slope_ref[:, cols].astype(F32)).astype(BF16)
        du_ref[0, :, cols] = up_grad
        add(UP_BIAS + i, row_sum(up_grad.astype(F32)))
        hidden_grad = hidden_grad + nn(up_grad, wf_ref[0, cols])
    add(GAIN1, row_sum(hidden_grad * unit1))
    add(SHIFT1, row_sum(hidden_grad))
    branch_grad = normalized_back(hidden_grad * row(GAIN1), unit1, inverse1).astype(BF16)
    da_ref[0] = branch_grad
    add(OUT_BIAS, row_sum(branch_grad.astype(F32)))
    for side in range(2):
        dc_ref[0, :, HALF * side : HALF * (side + 1)] = nn(branch_grad, wo_ref[side, 0]).astype(BF16)


def rows_part(x, c, cot, attn, ffn, table):
    rows = pl.BlockSpec((1, TILE, D), lambda s, i: (s, i, 0))
    wide = pl.BlockSpec((1, TILE, FF), lambda s, i: (s, i, 0))
    whole, whole_wide = sds((LOCAL, SEG, D), BF16), sds((LOCAL, SEG, FF), BF16)
    return pl.pallas_call(
        rows_kernel,
        grid=(LOCAL, SEG // TILE),
        in_specs=[rows] * 3
        + [once((2, 1, D, HALF), (0, 3, 0, 0)), once((2, FF, D), (0, 0, 0)), once((NVEC, D), (0, 0))],
        out_specs=[rows, rows, wide, wide, rows, rows, rows, once((THIN, D), (0, 0))],
        out_shape=[whole, whole, whole_wide, whole_wide, whole, whole, whole, sds((THIN, D), F32)],
        scratch_shapes=[pltpu.VMEM((TILE, FF), BF16)],
        compiler_params=params(),
    )(x, c, cot, attn, ffn, table)


def chain_back_kernel(
    place_ref,
    flag_ref,
    start_ref,
    table_ref,
    attn_ref,
    ffn_ref,
    q_ref,
    k_ref,
    v_ref,
    saved_d_ref,
    saved_f_ref,
    saved_s_ref,
    dk_in,
    dv_in,
    thin_d_in,
    thin_f_in,
    sums_in,
    dk_ref,
    dv_ref,
    thin_d_ref,
    thin_f_ref,
    sums_ref,
    grad_ref,
    wa,
    wf,
    qb,
    kb,
    vb,
    dkb,
    dvb,
    save_d,
    save_f,
    save_s,
    thin_d,
    thin_f,
    sums,
    sem_w,
    sem_in,
    sem_out,
):
    del dk_in, dv_in, thin_d_in, thin_f_in, sums_in
    grad_ref[...] = start_ref[...]

    @pl.when(flag_ref[0] > 0)
    def _():
        loads = [
            pltpu.make_async_copy(attn_ref, wa, sem_w.at[0]),
            pltpu.make_async_copy(ffn_ref.at[0], wf.at[0], sem_w.at[1]),
            pltpu.make_async_copy(ffn_ref.at[1], wf.at[1], sem_w.at[2]),
        ]
        reads = [
            pltpu.make_async_copy(q_ref.at[:, pl.ds(0, THIN)], qb, sem_in.at[0]),
            pltpu.make_async_copy(k_ref, kb, sem_in.at[1]),
            pltpu.make_async_copy(v_ref, vb, sem_in.at[2]),
            pltpu.make_async_copy(dk_ref, dkb, sem_in.at[3]),
            pltpu.make_async_copy(dv_ref, dvb, sem_in.at[4]),
            pltpu.make_async_copy(saved_d_ref, save_d, sem_in.at[5]),
            pltpu.make_async_copy(saved_f_ref, save_f, sem_in.at[6]),
            pltpu.make_async_copy(saved_s_ref, save_s, sem_in.at[7]),
        ]
        for c in reads + [loads[2], loads[1], loads[0]]:
            c.start()
        sums[...] = jnp.zeros_like(sums)
        masks = head_masks()
        memory_row = lax.broadcasted_iota(jnp.int32, (THIN, 1), 0) < MEM
        row = lambda r: table_ref[r : r + 1, :]

        def add(r, value):
            sums[r : r + 1, :] += value

        for c in reads:
            c.wait()
        loads[2].wait()
        loads[1].wait()
        loads[0].wait()
        for s in reversed(range(LOCAL)):
            after = flag_ref[2] if s == LOCAL - 1 else place_ref[s + 1]

            def through(s=s, after=after):
                grad = jnp.where(memory_row & (after > 0), grad_ref[...], 0.0)
                unit1, unit2 = save_d[s, 1].astype(F32), save_d[s, 2].astype(F32)
                base = HEADS * THIN
                log_total = save_s[s, 0:base, 0:1]
                inverse1 = save_s[s, base : base + THIN, 0:1]
                inverse2 = save_s[s, base + THIN :, 0:1]
                add(GAIN2, row_sum(grad * unit2))
                add(SHIFT2, row_sum(grad))
                second_grad = normalized_back(grad * row(GAIN2), unit2, inverse2)
                down_grad = second_grad.astype(BF16)
                add(DOWN_BIAS, row_sum(down_grad.astype(F32)))
                up_grad = (nt(down_grad, wf[1]) * save_f[s, 1].astype(F32)).astype(BF16)
                up_sum = row_sum(up_grad.astype(F32))
                for i in range(FF // D):
                    add(UP_BIAS + i, up_sum[:, D * i : D * (i + 1)])
                hidden_grad = second_grad + nn(up_grad, wf[0])
                add(GAIN1, row_sum(hidden_grad * unit1))
                add(SHIFT1, row_sum(hidden_grad))
                pre_grad = normalized_back(hidden_grad * row(GAIN1), unit1, inverse1)
                branch_grad = pre_grad.astype(BF16)
                add(OUT_BIAS, row_sum(branch_grad.astype(F32)))
                context_grad = jnp.concatenate(
                    [nn(branch_grad, wa[0, 3]), nn(branch_grad, wa[1, 3])], axis=1
                ).astype(BF16)
                dc_heads = by_head(context_grad, masks)
                q_heads = by_head(qb[s], masks)
                score = nt(q_heads, kb[s])
                share = jnp.exp(score - log_total) * copies_of(score.shape)
                share_grad = nt(dc_heads, vb[s])
                inner = jnp.sum(share_grad * share, axis=-1, keepdims=True)
                score_grad = (share * (share_grad - inner)).astype(BF16)
                query_grad = (own_columns(nn(score_grad, kb[s]), masks) * SCALE).astype(BF16)
                dkb[s] = (dkb[s].astype(F32) + tn(score_grad, q_heads)).astype(BF16)
                dvb[s] = (dvb[s].astype(F32) + tn(share.astype(BF16), dc_heads)).astype(BF16)
                thin_d[s, 0] = down_grad
                thin_d[s, 1] = branch_grad
                thin_d[s, 2] = query_grad
                thin_d[s, 3] = save_d[s, 0]
                thin_d[s, 4] = save_d[s, 3]
                thin_f[s, 0] = up_grad
                thin_f[s, 1] = save_f[s, 0]
                grad_ref[...] = (
                    pre_grad
                    + nt(query_grad[:, :HALF], wa[0, 0])
                    + nt(query_grad[:, HALF:], wa[1, 0])
                )

            if s == LOCAL - 1:

                @pl.when(flag_ref[1] > 0)
                def _():
                    through()

                @pl.when(flag_ref[1] == 0)
                def _():
                    thin_d[s] = jnp.zeros_like(thin_d[s])
                    thin_f[s] = jnp.zeros_like(thin_f[s])
                    grad_ref[...] = jnp.zeros_like(grad_ref)
            else:
                through()
            grad = grad_ref[...]
            for side in range(2):
                cols = slice(HALF * side, HALF * (side + 1))
                grad = grad + nt(dkb[s, 0:THIN, cols], wa[side, 1])
                grad = grad + nt(dvb[s, 0:THIN, cols], wa[side, 2])
            grad_ref[...] = grad
            first = jnp.where(place_ref[s] == 0, grad, 0.0)
            sums[FIRST_MEMORY : FIRST_MEMORY + THIN, :] += first
        writes = [
            pltpu.make_async_copy(dkb, dk_ref, sem_out.at[0]),
            pltpu.make_async_copy(dvb, dv_ref, sem_out.at[1]),
            pltpu.make_async_copy(thin_d, thin_d_ref, sem_out.at[2]),
            pltpu.make_async_copy(thin_f, thin_f_ref, sem_out.at[3]),
            pltpu.make_async_copy(sums, sums_ref, sem_out.at[4]),
        ]
        for c in writes:
            c.start()
        for c in writes:
            c.wait()


THIN_SHAPES = (
    sds((LOCAL, 5, THIN, D), BF16),
    sds((LOCAL, 2, THIN, FF), BF16),
    sds((FIRST_MEMORY + THIN, D), F32),
)


def chain_back(place, flag, start, table, attn, ffn, q, k, v, saved, dk, dv, thin):
    whole = sds((LOCAL, SEG, D), BF16)
    outs = pl.pallas_call(
        chain_back_kernel,
        in_specs=[SMEM, SMEM, VMEM, VMEM] + [ANY] * 13,
        out_specs=[ANY] * 5 + [VMEM],
        out_shape=[whole] * 2 + list(THIN_SHAPES) + [sds((THIN, D), F32)],
        input_output_aliases={12 + i: i for i in range(5)},
        scratch_shapes=[
            pltpu.VMEM((2, 4, D, HALF), BF16),
            pltpu.VMEM((2, FF, D), BF16),
            pltpu.VMEM((LOCAL, THIN, D), BF16),
        ]
        + [pltpu.VMEM((LOCAL, SEG, D), BF16)] * 4
        + [pltpu.VMEM(s.shape, s.dtype) for s in SAVED + THIN_SHAPES]
        + [
            pltpu.SemaphoreType.DMA((3,)),
            pltpu.SemaphoreType.DMA((8,)),
            pltpu.SemaphoreType.DMA((5,)),
        ],
        compiler_params=params(),
    )(place, flag, start, table, attn, ffn, q, k, v, *saved, dk, dv, *thin)
    return outs[:2], outs[2:5], outs[5]


def token_grad_kernel(da_ref, dq_ref, dk_ref, dv_ref, w_ref, out_ref):
    total = da_ref[0].astype(F32)
    for side in range(2):
        cols = slice(HALF * side, HALF * (side + 1))
        for i, ref in enumerate((dq_ref, dk_ref, dv_ref)):
            total = total + nt(ref[0, :, cols], w_ref[side, i])
    out_ref[0] = total.astype(BF16)


def token_gradient(da, dq, dk, dv, attn):
    rows = pl.BlockSpec((1, TILE, D), lambda s, i: (s, i, 0))
    return pl.pallas_call(
        token_grad_kernel,
        grid=(LOCAL, SEG // TILE),
        in_specs=[rows] * 4 + [once((2, 3, D, HALF), (0, 0, 0, 0))],
        out_specs=rows,
        out_shape=sds((LOCAL, SEG, D), BF16),
        compiler_params=params(),
    )(da, dq, dk, dv, attn)


def flat(ref):
    return ref[...].reshape(LOCAL * ref.shape[1], ref.shape[2])


def ffn_grad_kernel(g_ref, du_ref, df_ref, h_ref, thin_f_ref, thin_d_ref, out_ref):
    up = tn(flat(du_ref), flat(h_ref))
    down = tn(flat(g_ref), flat(df_ref))
    for s in range(LOCAL):
        up = up + tn(thin_f_ref[s, 0], thin_d_ref[s, 3])
        down = down + tn(thin_f_ref[s, 1], thin_d_ref[s, 0])
    out_ref[0] = up.astype(BF16)
    out_ref[1] = down.astype(BF16)


def ffn_gradient(g, du, df, h, thin_d, thin_f, chunk=256):
    hidden = pl.BlockSpec((LOCAL, SEG, chunk), lambda i: (0, 0, i))
    full = once((LOCAL, SEG, D), (0, 0, 0))
    return pl.pallas_call(
        ffn_grad_kernel,
        grid=(FF // chunk,),
        in_specs=[
            hidden,
            hidden,
            full,
            full,
            pl.BlockSpec((LOCAL, 2, THIN, chunk), lambda i: (0, 0, 0, i)),
            once(THIN_SHAPES[0].shape, (0, 0, 0, 0)),
        ],
        out_specs=pl.BlockSpec((2, chunk, D), lambda i: (0, i, 0)),
        out_shape=sds((2, FF, D), BF16),
        compiler_params=params(),
    )(g, du, df, h, thin_f, thin_d)


def attn_grad_kernel(x_ref, da_ref, dq_ref, dk_ref, dv_ref, c_ref, thin_d_ref, out_ref, bias_ref):
    thin_c = pl.ds(pl.multiple_of(pl.program_id(0) * HALF, HALF), HALF)
    x = flat(x_ref)
    dq, dk, dv = flat(dq_ref), flat(dk_ref), flat(dv_ref)
    query = tn(x, dq)
    query_bias = row_sum(dq.astype(F32))
    output = tn(flat(da_ref), flat(c_ref))
    for s in range(LOCAL):
        dq16 = thin_d_ref[s, 2, :, thin_c]
        query = query + tn(x_ref[s, 0:THIN], dq16)
        query_bias = query_bias + row_sum(dq16.astype(F32))
        output = output + tn(thin_d_ref[s, 1], thin_d_ref[s, 4, :, thin_c])
    out_ref[0, 0] = query.astype(BF16)
    out_ref[0, 1] = tn(x, dk).astype(BF16)
    out_ref[0, 2] = tn(x, dv).astype(BF16)
    out_ref[0, 3] = output.astype(BF16)
    bias_ref[0] = jnp.concatenate(
        [query_bias, row_sum(dv.astype(F32)), jnp.zeros((6, HALF), F32)], axis=0
    )


def attn_gradient(x, da, dq, dk, dv, c, thin_d):
    half = pl.BlockSpec((LOCAL, SEG, HALF), lambda i: (0, 0, i))
    full = once((LOCAL, SEG, D), (0, 0, 0))
    return pl.pallas_call(
        attn_grad_kernel,
        grid=(2,),
        in_specs=[full, full, half, half, half, half, once(THIN_SHAPES[0].shape, (0, 0, 0, 0))],
        out_specs=[
            pl.BlockSpec((1, 4, D, HALF), lambda i: (i, 0, 0, 0)),
            pl.BlockSpec((1, 8, HALF), lambda i: (i, 0, 0)),
        ],
        out_shape=[sds((2, 4, D, HALF), BF16), sds((2, 8, HALF), F32)],
        compiler_params=params(),
    )(x, da, dq, dk, dv, c, thin_d)


def update(gradient, momentum, weight, average, rate, grad_scale):
    scaled = gradient * grad_scale
    moment = MOMENTUM * momentum + scaled
    weight_new = weight - rate * (scaled + MOMENTUM * moment)
    return (moment, weight_new, AVERAGE_DECAY * average + (1.0 - AVERAGE_DECAY) * weight_new)


def gather_weights(attention, feedforward, vectors):
    attn = lax.all_gather(attention.astype(BF16), "dp", axis=1, tiled=True)
    attn = lax.all_gather(attn, "tensor", axis=0)
    hidden_major = jnp.swapaxes(feedforward.astype(BF16), 1, 2)
    ffn = lax.all_gather(hidden_major, ("dp", "tensor"), axis=1, tiled=True)
    table = lax.all_gather(vectors.astype(BF16), ("dp", "tensor"), axis=0, tiled=True)
    return attn, ffn, table.reshape(NVEC, D).astype(F32)


def swap(value):
    return lax.ppermute(value, "tensor", [(0, 1), (1, 0)])


def whole_rows(halves, side):
    mine = lax.dynamic_slice_in_dim(halves, LOCAL * side, LOCAL, 0)
    other = swap(lax.dynamic_slice_in_dim(halves, LOCAL * (1 - side), LOCAL, 0))
    first = jnp.where(side == 0, mine, other)
    second = jnp.where(side == 0, other, mine)
    return jnp.concatenate([jnp.zeros((LOCAL, MEM, D), halves.dtype), first, second], axis=1)


def half_rows(rows, side):
    half = (SEG - MEM) // 2
    first, second = rows[:, MEM : MEM + half], rows[:, MEM + half :]
    mine = jnp.where(side == 0, first, second)
    other = swap(jnp.where(side == 0, second, first))
    return jnp.concatenate(
        [jnp.where(side == 0, mine, other), jnp.where(side == 0, other, mine)], axis=0
    )


def on_device(
    tokens,
    slot_position,
    cotangent,
    attention,
    feedforward,
    vectors,
    attn_momentum,
    ffn_momentum,
    vec_momentum,
    attn_average,
    ffn_average,
    vec_average,
):
    side = lax.axis_index("tensor")
    first_side = side == 0
    attn, ffn, table = gather_weights(attention, feedforward, vectors)
    place = lax.dynamic_slice_in_dim(slot_position, LOCAL * side, LOCAL, 0)
    live = (place >= 0)[:, None, None]

    x = whole_rows(tokens, side)
    cot = jnp.where(live, whole_rows(cotangent, side), 0)
    q, k, v = project(x, attn, table)

    on = lambda flag: flag.astype(jnp.int32)
    saved = tuple(jnp.zeros(s.shape, s.dtype) for s in SAVED)
    start = jnp.zeros((THIN, D), BF16)
    flag = jnp.stack([on(first_side), jnp.int32(1)])
    (x, q, k, v), saved, memory = chain(place, flag, start, table, attn, ffn, x, q, k, v, saved)
    memory = lax.ppermute(memory, "tensor", [(0, 1)])
    flag = jnp.stack([on(~first_side), jnp.int32(0)])
    (x, q, k, v), saved, _ = chain(place, flag, memory, table, attn, ffn, x, q, k, v, saved)

    c, log_total = attend(q, k, v)
    y, h, g, du, df, da, dc, sums = rows_part(x, c, cot, attn, ffn, table)
    dq, dk, dv = attend_back(q, k, v, dc, log_total)

    thin = tuple(jnp.zeros(s.shape, s.dtype) for s in THIN_SHAPES)
    back = functools.partial(chain_back, place)
    flag = jnp.stack([on(~first_side), jnp.int32(0), jnp.int32(-1)])
    start = jnp.zeros((THIN, D), F32)
    (dk, dv), thin, grad = back(flag, start, table, attn, ffn, q, k, v, saved, dk, dv, thin)
    grad = lax.ppermute(grad, "tensor", [(1, 0)])
    flag = jnp.stack([on(first_side), jnp.int32(1), slot_position[LOCAL]])
    (dk, dv), thin, _ = back(flag, grad, table, attn, ffn, q, k, v, saved, dk, dv, thin)
    thin_d, thin_f, thin_sums = thin

    token_grad = token_gradient(da, dq, dk, dv, attn)
    ffn_terms = ffn_gradient(g, du, df, h, thin_d, thin_f)
    attn_terms, bias_terms = attn_gradient(x, da, dq, dk, dv, c, thin_d)

    activations = half_rows(jnp.where(live, y, 0), side)
    token_grad = half_rows(jnp.where(live, token_grad, 0), side)

    bias_rows = jnp.concatenate([bias_terms[0, :2], bias_terms[1, :2]], axis=1)
    leading = jnp.concatenate([bias_rows, sums[2:FIRST_MEMORY], jnp.zeros((MEM, D), F32)], axis=0)
    vec_terms = leading + thin_sums[:NVEC]

    attn_grad = lax.psum_scatter(attn_terms, "tensor", scatter_dimension=0, tiled=False)
    attn_grad = lax.psum_scatter(attn_grad, "dp", scatter_dimension=1, tiled=True).astype(F32)
    ffn_grad = lax.psum_scatter(ffn_terms, ("dp", "tensor"), scatter_dimension=1, tiled=True)
    ffn_grad = jnp.swapaxes(ffn_grad, 1, 2).astype(F32)
    vec_grad = lax.psum_scatter(
        vec_terms.reshape(-1), ("dp", "tensor"), scatter_dimension=0, tiled=True
    )
    grad_scale = 1.0 / math.sqrt(lax.axis_size("dp") * SLOTS * ROWS)
    attn_new = update(attn_grad, attn_momentum, attention, attn_average, ATTENTION_RATE, grad_scale)
    ffn_new = update(ffn_grad, ffn_momentum, feedforward, ffn_average, FEEDFORWARD_RATE, grad_scale)
    vec_new = update(vec_grad, vec_momentum, vectors, vec_average, VECTOR_RATE, grad_scale)
    return (
        activations,
        token_grad,
        attn_new[0],
        ffn_new[0],
        vec_new[0],
        attn_new[1],
        ffn_new[1],
        vec_new[1],
        attn_new[2],
        ffn_new[2],
        vec_new[2],
    )


def solution(mesh):
    attn_spec = P(None, "dp", "tensor")
    ffn_spec = P(None, None, ("dp", "tensor"))
    vec_spec = P(("dp", "tensor"))
    rows_spec = P("dp", "tensor", None)
    states = (attn_spec, ffn_spec, vec_spec)
    return jax.shard_map(
        on_device,
        mesh=mesh,
        in_specs=(rows_spec, P("dp"), rows_spec) + states * 3,
        out_specs=(rows_spec, rows_spec) + states * 3,
        check_vma=False,
    )
```

time: 1490 us -> 820 us (0.55)
  matrix products: 414 us -> 0 us
  local copies, waits for them, and re-layouts: 217 us -> 27 us
  Pallas kernels: 0 us -> 181 us
  blocking collectives: 195 us -> 91 us
  other arithmetic: 104 us -> 23.9 us
  loops' own time: 38.6 us -> 0 us
  starting transfers between devices: 26.7 us -> 5.7 us
    dot_general x76 -> x0, matrix products: 414 us -> none  [the longest x4 66 us: backward_slot(): jnp.einsum('hqk,khd->qhd', raw_grad, split_heads[:, 1], preferred_element...]
    pallas_call x0 -> x11, Pallas kernels: none -> 181 us  [the longest x1 42.9 us: rows_part(): pl.pallas_call(rows_kernel, grid=(LOCAL, SEG // TILE), in_specs=[rows] *...]
    while x8 -> x0, blocking collectives: 85.1 us -> none
    all_gather x8 -> x0, blocking collectives: 68.4 us -> none  [the longest x4 37.1 us: forward_slot(): all_rows = lax.all_gather(local_rows, 'tensor', axis=0, tiled=True)]
    reduce_scatter x2 -> x3, waiting for transfers between devices: 287 us -> 232 us  [the longest x1 132 us: on_device(): lax.psum_scatter(ffn_terms, ('dp', 'tensor'), scatter_dimension=1, tiled=...]
    unnamed x1, blocking collectives: 41.9 us -> 91 us
    unnamed x40 -> x38, local copies, waits for them, and re-layouts: 54.5 us -> 8.28 us
    while x275 -> x0, local copies, waits for them, and re-layouts: 40.8 us -> none  [the longest x3 24.5 us: on_device(): lax.scan(backward_slot, start_carry, (stored_all, slot_position, cotangen...]
  transfers between devices with their start and end apart: 21 -> 13, of which waited for: 4 -> 7; matrix products, arithmetic and copies ran while one was open for 14% -> 5% of each run, Pallas kernels for 0% -> 5%
where the time goes in v1:
time: 820 us; the launch traced here: 807 us
  waiting for transfers between devices  464 us (57%)
  Pallas kernels  181 us (22%)
  blocking collectives  91 us (11%)
  local copies, waits for them, and re-layouts  27 us (3%)
  other arithmetic  23.9 us (3%)
  between operations  14.6 us (2%)
    reduce_scatter x1, waiting for transfers between devices, on_device(): lax.psum_scatter(ffn_terms, ('dp', 'tensor'), scatter_dimension=1, tiled=...  132 us
    unnamed x8, waiting for transfers between devices  110 us
    unnamed x1, blocking collectives  91 us
    reduce_scatter x1, waiting for transfers between devices, on_device(): lax.psum_scatter(attn_grad, 'dp', scatter_dimension=1, tiled=True)  64 us
    all_gather x1, waiting for transfers between devices, gather_weights(): ffn = lax.all_gather(hidden_major, ('dp', 'tensor'), axis=1, tiled=True)  57.3 us
    all_gather x1, waiting for transfers between devices, gather_weights(): attn = lax.all_gather(attention.astype(BF16), 'dp', axis=1, tiled=True)  46.7 us
    pallas_call x1, Pallas kernels, rows_part(): pl.pallas_call(rows_kernel, grid=(LOCAL, SEG // TILE), in_specs=[rows] *...  42.9 us
    reduce_scatter x1, waiting for transfers between devices, on_device(): lax.psum_scatter(attn_terms, 'tensor', scatter_dimension=0, tiled=False)  36.4 us
  transfers between devices with their start and end apart: 13, of which 7 were waited for; matrix products, arithmetic and copies ran while one was open for 5% of the time, Pallas kernels for 5%

profile of v1, /device:TPU:1, one launch (start us, length us, event | category | flops | bytes accessed | tf_op | source)
XLA Modules:
  0.0 807.3 jit_solution(18432081743990806583)
XLA Ops:
  9.0 46.7 %all-gather.5.cloned.1.call-done = bf16[4,768,384]{2,1,0:T(8,128)(2,1)} async-done(((bf16[4,48,384]{2,1,0:T(8,128)(2,1)}), bf16[4,768,384]{2,1,0:T(8,128)(2,1)}) %all-gather.5.cloned.1.call-update) | async-done | bytes 2359312 | tf_op jit(solution)/shard_map/all_gather | solution.py:809
  57.3 2.5 constant_dynamic-slice_fusion
  60.9 4.7 constant_dynamic-slice_fusion.2
  65.9 91.0 %all-reduce = bf16[16896]{0:T(1024)(128)(2,1)S(1)} all-reduce(bf16[16896]{0:T(1024)(128)(2,1)S(1)} %dynamic-update-slice), channel_id=1, replica_groups=mesh['dp'=16,'tensor'=2] {'dp','tensor'}, use_global_device_ids=true, to_apply=%add | all-reduce | flops 16896 | bytes 67584
  163.0 2.9 maximum_select_fusion
  165.9 8.6 %shard_map.203 = (bf16[2,512,768]{2,1,0:T(8,128)(2,1)}, bf16[2,512,768]{2,1,0:T(8,128)(2,1)}, bf16[2,512,768]{2,1,0:T(8,128)(2,1)}) custom-call(bf16[2,512,768]{2,1,0:T(8,128)(2,1)} %get-tuple-element.147.x_ref.x_in, bf16[2,4,768,384]{3,2,1,0:T(8,128)(2,1)} %bitcast.19, f32[22,768]{1,0:T(8,128)} %reshape.32.table_ref), custom_call_target="tpu_custom_call" | custom-call | tf_op jit(solution)/shard_map/pallas_call | solution.py:119
  174.5 57.3 %all-gather.7.cloned.1.call-done.ffn_ref.wf_ref = bf16[2,3072,768]{2,1,0:T(8,128)(2,1)} async-done(((bf16[2,96,768]{2,1,0:T(8,128)(2,1)}), bf16[2,3072,768]{2,1,0:T(8,128)(2,1)}) %all-gather.7.cloned.1.call-update) | async-done | bytes 9437200 | tf_op jit(solution)/shard_map/all_gather | solution.py:812
  234.6 14.9 %shard_map.204 = (bf16[2,512,768]{2,1,0:T(8,128)(2,1)}, bf16[2,512,768]{2,1,0:T(8,128)(2,1)}, bf16[2,512,768]{2,1,0:T(8,128)(2,1)}, bf16[2,512,768]{2,1,0:T(8,12...) custom-call(s32[2]{0:T(128)} %get-tuple-element.131.place_ref, ...), custom_call_target="tpu_custom_call", output_to_operand_aliasing={{0}: (6, {}), {1}: (7, {}), {2}: (8, {}), {3}: (9, {}), {4}... | custom-call | tf_op jit(solution)/shard_map/pallas_call | solution.py:316
  252.7 8.8 %shard_map.205 = (bf16[2,512,768]{2,1,0:T(8,128)(2,1)}, bf16[2,512,768]{2,1,0:T(8,128)(2,1)}, bf16[2,512,768]{2,1,0:T(8,128)(2,1)}, bf16[2,512,768]{2,1,0:T(8,12...) custom-call(s32[2]{0:T(128)} %get-tuple-element.131.place_ref, ...), custom_call_target="tpu_custom_call", output_to_operand_aliasing={{0}: (6, {}), {1}: (7, {}), {2}: (8, {}), {3}: (9, {}), {4}... | custom-call | tf_op jit(solution)/shard_map/pallas_call | solution.py:316
  261.6 16.8 %shard_map.206 = (bf16[2,512,768]{2,1,0:T(8,128)(2,1)}, f32[2,6,2,512]{3,2,1,0:T(2,128)}) custom-call(bf16[2,512,768]{2,1,0:T(8,128)(2,1)} %get-tuple-element.67.q_ref, bf16[2,512,768]{2,1,0:T(8,128)(2,1)} %get-tuple-element.68.k_ref, bf16[2,512,768]{2,1,0:T(8,128)(2,1)} %get-tuple-element.69.v_ref), custom_call_target="tpu_custom_call" | custom-call | tf_op jit(solution)/shard_map/pallas_call | solution.py:376
  278.3 42.9 %shard_map.207 = (bf16[2,512,768]{2,1,0:T(8,128)(2,1)}, bf16[2,512,768]{2,1,0:T(8,128)(2,1)}, bf16[2,512,3072]{2,1,0:T(8,128)(2,1)}, bf16[2,512,3072]{2,1,0:T(8,...) custom-call(bf16[2,512,768]{2,1,0:T(8,128)(2,1)} %get-tuple-element., ...), custom_call_target="tpu_custom_call" | custom-call | tf_op jit(solution)/shard_map/pallas_call | solution.py:504
  321.2 24.1 %shard_map.208 = (bf16[2,512,768]{2,1,0:T(8,128)(2,1)}, bf16[2,512,768]{2,1,0:T(8,128)(2,1)}, bf16[2,512,768]{2,1,0:T(8,128)(2,1)}) custom-call(bf16[2,512,768]{2,1,0:T(8,128)(2,1)} %get-tuple-element.67.q_ref, bf16[2,512,768]{2,1,0:T(8,128)(2,1)} %get-tuple-element.68.k_ref, bf16[2,512,768]{2,1,0:T(8,128)(2,1)} %get-tuple-element.69.v_ref, ...), custom_call_target="tpu_custom_call" | custom-call | tf_op jit(solution)/shard_map/pallas_call | solution.py:424
  352.7 18.5 %collective-permute-done.4.start_ref = f32[16,768]{1,0:T(8,128)S(1)} collective-permute-done((f32[16,768]{1,0:T(8,128)}, f32[16,768]{1,0:T(8,128)S(1)}, u32[]{:S(2)}, u32[]{:S(2)}) %collective-permute-start.4) | collective-permute-done | bytes 49184 | tf_op jit(solution)/shard_map/ppermute | solution.py:881
  371.8 19.8 %shard_map.210 = (bf16[2,512,768]{2,1,0:T(8,128)(2,1)}, bf16[2,512,768]{2,1,0:T(8,128)(2,1)}, bf16[2,5,16,768]{3,2,1,0:T(8,128)(2,1)}, bf16[2,2,16,3072]{3,2,1,0...) custom-call(s32[2]{0:T(128)} %get-tuple-element.131.place_ref, ...), custom_call_target="tpu_custom_call", output_to_operand_aliasing={{0}: (12, {}), {1}: (13, {}), {2}: (14, {}), {3}: (15, {}),... | custom-call | tf_op jit(solution)/shard_map/pallas_call | solution.py:686
  391.6 12.7 %shard_map.212 = (bf16[2,4,768,384]{3,2,1,0:T(8,128)(2,1)}, f32[2,8,384]{2,1,0:T(8,128)}) custom-call(bf16[2,512,768]{2,1,0:T(8,128)(2,1)} %get-tuple-element.66.x_ref, bf16[2,512,768]{2,1,0:T(8,128)(2,1)} %get-tuple-element.72.da_ref, bf16[2,512,768]{2,1,0:T(8,128)(2,1)} %get-tuple-element.75.dq_ref, bf16[2,512,768]{2,1,0:T(8,128)(2,1)} %get-tuple-element.87.dk_ref, ...), custom_call_target="tpu_custom_call" | custom-call | tf_op jit(solution)/shard_map/pallas_call | solution.py:788
  406.6 21.1 %shard_map.213 = bf16[2,3072,768]{2,1,0:T(8,128)(2,1)} custom-call(bf16[2,512,3072]{2,1,0:T(8,128)(2,1)} %get-tuple-element.91.g_ref, bf16[2,512,3072]{2,1,0:T(8,128)(2,1)} %get-tuple-element.92.du_ref, bf16[2,512,768]{2,1,0:T(8,128)(2,1)} %get-tuple-element.93.df_ref, bf16[2,512,768]{2,1,0:T(8,128)(2,1)} %get-tuple-element.94.h_ref, ...), custom_call_target="tpu_custom_call" | custom-call | tf_op jit(solution)/shard_map/pallas_call | solution.py:747
  428.0 36.4 %reduce-scatter.4.cloned.1.call-done = bf16[1,4,768,384]{3,2,1,0:T(8,128)(2,1)} async-done(((bf16[2,4,768,384]{3,2,1,0:T(8,128)(2,1)}), bf16[1,4,768,384]{3,2,1,0:T(8,128)(2,1)}) %reduce-scatter.4.cloned.1.call-update) | async-done | bytes 2359312 | tf_op jit(solution)/shard_map/reduce_scatter | solution.py:897
  464.3 9.0 %shard_map.211 = bf16[2,512,768]{2,1,0:T(8,128)(2,1)} custom-call(bf16[2,512,768]{2,1,0:T(8,128)(2,1)} %get-tuple-element.72.da_ref, bf16[2,512,768]{2,1,0:T(8,128)(2,1)} %get-tuple-element.75.dq_ref, bf16[2,512,768]{2,1,0:T(8,128)(2,1)} %get-tuple-element.87.dk_ref, bf16[2,512,768]{2,1,0:T(8,128)(2,1)} %get-tuple-element.88.dv_ref, ...), custom_call_target="tpu_custom_call" | custom-call | tf_op jit(solution)/shard_map/pallas_call | solution.py:720
  481.1 109.6 %all-reduce.4.cloned.1.call-done = f32[16896]{0:T(1024)} async-done(((f32[16896]{0:T(1024)}), f32[16896]{0:T(1024)}) %all-reduce.4.cloned.1.call-update) | async-done | bytes 67600
  593.9 2.3 copy.65
  598.1 2.3 copy.66
  600.4 131.6 %reduce-scatter.8.cloned.1.call-done = bf16[2,96,768]{2,1,0:T(8,128)(2,1)} async-done(((bf16[2,3072,768]{2,1,0:T(8,128)(2,1)}), bf16[2,96,768]{2,1,0:T(8,128)(2,1)}) %reduce-scatter.8.cloned.1.call-update) | async-done | bytes 294928 | tf_op jit(solution)/shard_map/reduce_scatter | solution.py:899
  732.0 2.3 multiply_add_fusion
  734.4 64.0 %reduce-scatter.6.cloned.1.call-done = bf16[4,48,384]{2,1,0:T(8,128)(2,1)} async-done(((bf16[4,768,384]{2,1,0:T(8,128)(2,1)}), bf16[4,48,384]{2,1,0:T(8,128)(2,1)}) %reduce-scatter.6.cloned.1.call-update) | async-done | bytes 147472 | tf_op jit(solution)/shard_map/reduce_scatter | solution.py:898
  (102 shorter events, 41.8 us)
Async XLA Ops:
  7.2 48.6 %copy-start = (f32[2,768,96]{1,2,0:T(8,128)S(1)}, f32[2,768,96]{1,2,0:T(8,128)}, u32[]{:S(2)}) copy-start(f32[2,768,96]{1,2,0:T(8,128)} %param.16) | copy-start | bytes 1769476
  7.2 48.6 %all-gather.5.cloned.1.call-start = ((), (), s32[]{:S(2)}) async-start(), calls=%async_computation.3 | async-start | bytes 2506752 | tf_op jit(solution)/shard_map/all_gather | solution.py:809
  9.0 156.9 %all-gather.9.cloned.1.call-start = ((), (), s32[]{:S(2)}) async-start(), calls=%async_computation.8 | async-start | bytes 7077888 | tf_op jit(solution)/shard_map/all_gather | solution.py:810
  55.8 176.1 %all-gather.7.cloned.1.call-start = ((), (), s32[]{:S(2)}) async-start(), calls=%async_computation.4 | async-start | bytes 9732096 | tf_op jit(solution)/shard_map/all_gather | solution.py:812
  56.6 407.7 %reduce-scatter.4.cloned.1.call-start = ((), (), s32[]{:S(2)}) async-start(), calls=%async_computation.5 | async-start | bytes 7077888 | tf_op jit(solution)/shard_map/reduce_scatter | solution.py:897
  59.7 5.9 copy-start.13
  59.7 99.1 %copy-start.16 = (s32[4]{0:T(128)S(1)}, s32[4]{0:T(128)}, u32[]{:S(2)}) copy-start(s32[4]{0:T(128)} %param.13) | copy-start | bytes 52
  59.7 99.7 %collective-permute-start.2 = (bf16[2,251,768]{2,0,1:T(2,128)(2,1)}, bf16[2,251,768]{2,0,1:T(2,128)(2,1)S(1)}, u32[]{:S(2)}, u32[]{:S(2)}) collective-permute-start(bf16[2,251,768]{2,0,1:T(2,128)(2,1)} %get-tuple-element.138), channel_id=1, source_target_pairs={{0,1},{1,0},{2,3},{3,2},{4,5},{5,4},{6,7},{7,6},{8,9},{9,8},{10,11... | collective-permute-start | bytes 2313224 | tf_op jit(solution)/shard_map/ppermute | solution.py:818
  65.6 96.0 %collective-permute-start = (bf16[2,251,768]{2,0,1:T(2,128)(2,1)}, bf16[2,251,768]{2,0,1:T(2,128)(2,1)}, u32[]{:S(2)}, u32[]{:S(2)}) collective-permute-start(bf16[2,251,768]{2,0,1:T(2,128)(2,1)} %get-tuple-element.142), channel_id=1, source_target_pairs={{0,1},{1,0},{2,3},{3,2},{4,5},{5,4},{6,7},{7,6},{8,9},{9,8},{10,11... | collective-permute-start | bytes 2313224 | tf_op jit(solution)/shard_map/ppermute | solution.py:818
  249.6 2.6 collective-permute-start.1
  350.1 21.0 %collective-permute-start.4 = (f32[16,768]{1,0:T(8,128)}, f32[16,768]{1,0:T(8,128)S(1)}, u32[]{:S(2)}, u32[]{:S(2)}) collective-permute-start(f32[16,768]{1,0:T(8,128)} %get-tuple-element.81), channel_id=1, source_target_pairs={{1,0},{3,2},{5,4},{7,6},{9,8},{11,10},{13,12},{15,14},{17,16},{19,... | collective-permute-start | bytes 147464 | tf_op jit(solution)/shard_map/ppermute | solution.py:881
  404.3 186.4 %all-reduce.4.cloned.1.call-start = ((), (), s32[]{:S(2)}) async-start(), calls=%async_computation.9 | async-start | bytes 139264
  406.5 325.5 %reduce-scatter.8.cloned.1.call-start = ((), (), s32[]{:S(2)}) async-start(), calls=%async_computation.7 | async-start | bytes 9732096 | tf_op jit(solution)/shard_map/reduce_scatter | solution.py:899
  427.7 370.6 %reduce-scatter.6.cloned.1.call-start = ((), (), s32[]{:S(2)}) async-start(), calls=%async_computation.6 | async-start | bytes 2506752 | tf_op jit(solution)/shard_map/reduce_scatter | solution.py:898
  477.6 114.6 %collective-permute-start.3 = (bf16[2,251,768]{2,0,1:T(2,128)(2,1)}, bf16[2,251,768]{2,0,1:T(2,128)(2,1)}, u32[]{:S(2)}, u32[]{:S(2)}) collective-permute-start(bf16[2,251,768]{2,0,1:T(2,128)(2,1)} %copy.59), channel_id=1, source_target_pairs={{0,1},{1,0},{2,3},{3,2},{4,5},{5,4},{6,7},{7,6},{8,9},{9,8},{10,11... | collective-permute-start | bytes 2313224 | tf_op jit(solution)/shard_map/ppermute | solution.py:818
  477.8 113.0 %copy-start.14 = (f32[528]{0:T(1024)S(1)}, f32[528]{0:T(1024)}, u32[]{:S(2)}) copy-start(f32[528]{0:T(1024)} %param.23) | copy-start | bytes 6340
  477.8 113.0 %copy-start.15 = (f32[528]{0:T(1024)S(1)}, f32[528]{0:T(1024)}, u32[]{:S(2)}) copy-start(f32[528]{0:T(1024)} %param.20) | copy-start | bytes 6340
  479.8 116.4 %collective-permute-start.5 = (bf16[2,251,768]{2,0,1:T(2,128)(2,1)}, bf16[2,251,768]{2,0,1:T(2,128)(2,1)}, u32[]{:S(2)}, u32[]{:S(2)}) collective-permute-start(bf16[2,251,768]{2,0,1:T(2,128)(2,1)} %copy.62), channel_id=1, source_target_pairs={{0,1},{1,0},{2,3},{3,2},{4,5},{5,4},{6,7},{7,6},{8,9},{9,8},{10,11... | collective-permute-start | bytes 2313224 | tf_op jit(solution)/shard_map/ppermute | solution.py:818
  598.1 134.0 %copy-start.1 = (f32[2,768,96]{1,2,0:T(8,128)S(1)}, f32[2,768,96]{1,2,0:T(8,128)}, u32[]{:S(2)}) copy-start(f32[2,768,96]{1,2,0:T(8,128)} %param.16) | copy-start | bytes 1769476
  598.1 134.0 %copy-start.6 = (f32[2,768,96]{1,2,0:T(8,128)S(1)}, f32[2,768,96]{1,2,0:T(8,128)}, u32[]{:S(2)}) copy-start(f32[2,768,96]{1,2,0:T(8,128)} %param.22) | copy-start | bytes 1769476
  598.1 134.0 %copy-start.7 = (f32[2,768,96]{1,2,0:T(8,128)S(1)}, f32[2,768,96]{1,2,0:T(8,128)}, u32[]{:S(2)}) copy-start(f32[2,768,96]{1,2,0:T(8,128)} %param.19) | copy-start | bytes 1769476
  600.4 198.0 %copy-start.4 = (f32[4,48,384]{2,1,0:T(8,128)S(1)}, f32[4,48,384]{2,1,0:T(8,128)}, u32[]{:S(2)}) copy-start(f32[4,48,384]{2,1,0:T(8,128)} %param.15) | copy-start | bytes 884740
  600.4 198.0 %copy-start.8 = (f32[4,48,384]{2,1,0:T(8,128)S(1)}, f32[4,48,384]{2,1,0:T(8,128)}, u32[]{:S(2)}) copy-start(f32[4,48,384]{2,1,0:T(8,128)} %param.21) | copy-start | bytes 884740
  600.4 198.0 %copy-start.9 = (f32[4,48,384]{2,1,0:T(8,128)S(1)}, f32[4,48,384]{2,1,0:T(8,128)}, u32[]{:S(2)}) copy-start(f32[4,48,384]{2,1,0:T(8,128)} %param.18) | copy-start | bytes 884740
  (6 other events, 5.9 us)
Sparse Core Ops, SparseCore 0:
  10.8 44.9 all-gather.4
  57.3 89.8 all-gather.8
  150.8 81.0 all-gather.6
  404.4 59.8 reduce-scatter.3
  471.2 119.4 all-reduce.3
  597.5 134.4 reduce-scatter.7
  735.8 62.5 reduce-scatter.5
